TPU v7x, 256 devices: a whole 4x4x8 slice. The times are simulated.
256 devices in a mesh: beam: 8 (over z_hi, core), tile: 32 (over z_lo, x, y).
Axes of the slice: x: 4, y: 4, z: 8 (z_hi: 4, z_lo: 2; z = z_hi * 2 + z_lo), core: 2. Of those that a mesh axis runs over, the one named last changes fastest.
Arguments:
- model_grid: float32 [8, 2, 2048, 2048], P('beam', None, 'tile'), may hold values from -4 to 4
- observed: float32 [8, 2048, 2, 256], P('beam', 'tile'), may hold values from -6 to 6
- coords: float32 [8, 2048, 2, 256], P('beam', 'tile'), may hold values from 8 to 56
- vis_count: int32 [8, 32, 64], P('beam', 'tile'), may hold values from 1 to 256, 10240 in all within a row
- subgrid_block: int32 [8, 32, 64], P('beam', 'tile'), may hold values from 0 to 63, each once within a row
- subgrid_cell: int32 [8, 32, 64], P('beam', 'tile'), may hold values from 0 to 31
- beam_gain: float32 [8, 2048, 2048], P('beam', 'tile'), may hold values from 0.1 to 1
- column_shift: int32 [8], P('beam'), may hold values from 0 to 32
- row_offset: int32 [8], P('beam'), may hold values from 0 to 2048
- interp_index: int32 [8, 2], P('beam'), may hold values from 0 to 7
- interp_taps: float32 [8, 5], replicated, may hold values from 0.05 to 0.5
Outputs:
- gradient_sky: float32 [2, 2048, 4096], P(None, 'tile', 'beam')
Inputs may be any that keep to these rules, and one draw needn't show every extreme that they name: `vis_count`: in each slab of each beam the 64 counts sum to 10240 and the largest is 256. `subgrid_block`: each slab's row is a permutation.
All inputs are finite; a program needn't handle non-finite values.
Results may differ from a plain program's by a relative error of at most 0.00013.
Values sent between devices are 32-bit elements; how exact they have to be, the bound alone decides.
A program may use at most 64 MiB of HBM per device.

v0:
```python
import functools
import math

import jax
import jax.numpy as jnp
import numpy as np
from jax import lax
from jax.experimental import pallas as pl
from jax.experimental.pallas import tpu as pltpu
from jax.sharding import PartitionSpec as P

SIDE = 64
NT = 32
G = 2048
SLOTS = 256
SUBS = 64
SCALE = 3.0
PAD = 8
VMEM_LIMIT = 56 * 1024 * 1024
MESH = pl.DeviceIdType.MESH

f32 = jnp.float32
bf16 = jnp.bfloat16


def split_np(table):
    high = np.asarray(table, np.float32).astype(bf16)
    low = (np.asarray(table, np.float64) - high.astype(np.float64)).astype(np.float32).astype(bf16)
    return high, low


def row_tables():
    x1 = np.arange(NT)[:, None, None]
    x2 = np.arange(SIDE)[None, :, None]
    w = np.arange(SIDE)[None, None, :]
    angle = 2.0 * math.pi * ((w * (NT * x2 + x1)) % G) / G
    high, low = split_np(np.concatenate([np.cos(angle), np.sin(angle)], axis=1))
    return np.concatenate([high, high, low], axis=2)


def column_tables():
    y1 = np.arange(NT)[:, None, None]
    y2 = np.arange(SIDE)[None, :, None]
    r = np.arange(SIDE)[None, None, :]
    angle = 2.0 * math.pi * ((r * (NT * y2 + y1)) % G) / G
    high, low = split_np(np.concatenate([np.cos(angle), -np.sin(angle)], axis=2) / G)
    top = np.concatenate([high, high], axis=2)
    bottom = np.concatenate([low, np.zeros_like(low)], axis=2)
    return np.concatenate([top, bottom], axis=1)


def split(value):
    high = value.astype(bf16)
    low = (value - high.astype(f32)).astype(bf16)
    return high, low


def lane_signs(shape):
    lane = lax.broadcasted_iota(jnp.int32, shape, 1)
    return jnp.where(lane < SIDE, -1.0, 1.0).astype(f32)


def swapped(value):
    return pltpu.roll(value, SIDE, 1)


def transform(parts, signs):
    n = len(parts)
    if n == 1:
        return parts
    even = transform(parts[0::2], signs)
    odd = transform(parts[1::2], signs)
    low, high = [], []
    for k in range(n // 2):
        if k == 0:
            turned = odd[k]
        elif 4 * k == n:
            turned = swapped(odd[k]) * signs
        else:
            angle = 2.0 * math.pi * k / n
            turned = odd[k] * math.cos(angle) + swapped(odd[k]) * (signs * math.sin(angle))
        low.append(even[k] + turned)
        high.append(even[k] - turned)
    return low + high


def transform_leading(source, target):
    signs = lane_signs((8, 2 * SIDE))

    def tile(i, carry):
        at = pl.ds(pl.multiple_of(i * 8, 8), 8)
        for k, value in enumerate(transform([source[q, at, :] for q in range(NT)], signs)):
            target[k, at, :] = value
        return carry

    lax.fori_loop(0, SIDE // 8, tile, 0)


def grid_kernel(
    model, observed, coords, count, block, cell, shift, tap_index, taps, table, out,
    windows, grid, spectrum, padded, rising, falling,
):
    row = lax.broadcasted_iota(jnp.int32, (SIDE, 2 * SIDE), 0).astype(f32)
    rising[...] = jnp.exp(row / SCALE)
    falling[...] = jnp.exp(row / -SCALE)
    left = lax.broadcasted_iota(jnp.int32, (SIDE, 2 * SIDE), 1) < SIDE

    def prepare(pair, carry):
        at = pl.ds(pl.multiple_of(pair * 2 * SIDE, 2 * SIDE), 2 * SIDE)
        for plane in range(2):
            value = model[0, plane, :, at]
            high = value.astype(bf16).astype(f32)
            low = value - high
            rows = pl.ds(plane * SIDE, SIDE)
            windows[2 * pair, rows, :] = jnp.where(left, high, swapped(low)).astype(bf16)
            windows[2 * pair + 1, rows, :] = jnp.where(left, swapped(high), low).astype(bf16)
        return carry

    lax.fori_loop(0, NT // 2, prepare, 0)
    grid[...] = jnp.zeros_like(grid)
    slot = lax.broadcasted_iota(jnp.int32, (2, SLOTS), 1)

    def one(i):
        k = block[0, 0, i]
        q = cell[0, 0, i]
        position = coords[0, k]
        near = jnp.exp(position / -SCALE)
        far = jnp.exp(position / SCALE)
        up = jnp.concatenate([rising[...], rising[...]], axis=1)
        down = jnp.concatenate([falling[...], falling[...]], axis=1)
        along_v = jnp.minimum(up * near[0:1], down * far[0:1])
        along_u = jnp.minimum(up * near[1:2], down * far[1:2])
        high_u, low_u = split(along_u)
        window = windows[q]
        rows = jnp.dot(
            jnp.concatenate([window, window], axis=1),
            jnp.concatenate([high_u, high_u, low_u, low_u], axis=0),
            preferred_element_type=f32,
        )
        predicted = jnp.sum(rows.reshape(2, SIDE, SLOTS) * along_v[None], axis=1)
        residual = jnp.where(slot < count[0, 0, i], observed[0, k] - predicted, 0.0)
        weighted = jnp.concatenate([along_v * residual[0:1], along_v * residual[1:2]], axis=0)
        high_w, low_w = split(weighted)
        products = lax.dot_general(
            jnp.concatenate([high_u, low_u], axis=0),
            jnp.concatenate([high_w, low_w], axis=0),
            (((1,), (1,)), ((), ())),
            preferred_element_type=f32,
        )
        patch = products[:SIDE, : 2 * SIDE] + (
            products[SIDE:, : 2 * SIDE] + products[:SIDE, 2 * SIDE :]
        )
        return q, patch

    def several(i, carry):
        done = [one(i * 4 + j) for j in range(4)]
        for q, patch in done:
            grid[q] += patch
        return carry

    lax.fori_loop(0, SUBS // 4, several, 0)

    transform_leading(grid, spectrum)
    signs = lane_signs((SIDE, 2 * SIDE))
    padded[pl.ds(0, PAD), :] = jnp.zeros((PAD, 2 * SIDE), f32)
    padded[pl.ds(PAD + G, PAD), :] = jnp.zeros((PAD, 2 * SIDE), f32)
    for x1 in range(NT):
        high, low = split(spectrum[x1])
        both = jnp.dot(
            table[x1], jnp.concatenate([high, low, high], axis=0), preferred_element_type=f32
        )
        padded[pl.ds(PAD + x1, SIDE, stride=NT), :] = both[:SIDE] + swapped(both[SIDE:]) * signs

    phase = tap_index[0, 0]
    weights = [taps[phase, tap] for tap in range(5)]
    steps = shift[0]

    def send_block(d, carry):
        start = pl.multiple_of(d * SIDE, SIDE)
        total = weights[0] * padded[pl.ds(start + PAD + 2, SIDE), :]
        for tap in range(1, 5):
            total = total + weights[tap] * padded[pl.ds(start + PAD + 2 - tap, SIDE), :]
        out[(d + steps) % NT] = total
        return carry

    lax.fori_loop(0, NT, send_block, 0)


def image_kernel(columns, gain, offset, tap_index, taps, table, out, spectrum, padded, smooth):
    transform_leading(columns, spectrum)
    zeros = jnp.zeros((PAD, SIDE), f32)
    padded[pl.ds(0, PAD), pl.ds(0, SIDE)] = zeros
    padded[pl.ds(PAD + G, PAD), pl.ds(0, SIDE)] = zeros
    for y1 in range(NT):
        high, low = split(spectrum[y1])
        both = lax.dot_general(
            table[y1],
            jnp.concatenate([high, low], axis=1),
            (((1,), (1,)), ((), ())),
            preferred_element_type=f32,
        )
        padded[pl.ds(PAD + y1, SIDE, stride=NT), pl.ds(0, SIDE)] = both[:SIDE] + both[SIDE:]

    phase = tap_index[0, 1]
    weights = [taps[phase, tap] for tap in range(5)]
    for part in range(G // 128):
        total = weights[0] * padded[pl.ds(part * 128 + PAD + 2, 128), :]
        for tap in range(1, 5):
            total = total + weights[tap] * padded[pl.ds(part * 128 + PAD + 2 - tap, 128), :]
        turned = total.T[:SIDE]
        at = pl.ds(part * 128, 128)
        smooth[:, at] = turned * gain[0, :, at]
    out[...] = pltpu.roll(smooth[...], offset[0], 1)


def exchange_kernel(n, blocks, out, send_sem, recv_sem, own_sem):
    me = lax.axis_index("tile")
    barrier = pltpu.get_barrier_semaphore()
    for step in range(1, n):
        pl.semaphore_signal(
            barrier, inc=1, device_id={"tile": lax.rem(me + step, n)}, device_id_type=MESH
        )
    own = pltpu.make_async_copy(blocks.at[me], out.at[me], own_sem)
    own.start()
    pl.semaphore_wait(barrier, n - 1)
    copies = []
    for step in range(1, n):
        peer = lax.rem(me + step, n)
        copy = pltpu.make_async_remote_copy(
            src_ref=blocks.at[peer],
            dst_ref=out.at[me],
            send_sem=send_sem.at[step],
            recv_sem=recv_sem.at[step],
            device_id={"tile": peer},
            device_id_type=MESH,
        )
        copy.start()
        copies.append(copy)
    own.wait()
    for copy in copies:
        copy.wait()


SMEM = pl.BlockSpec(memory_space=pltpu.SMEM)
VMEM = pl.BlockSpec(memory_space=pltpu.VMEM)
ANY = pl.BlockSpec(memory_space=pl.ANY)


def gridded(model, observed, coords, count, block, cell, shift, tap_index, taps):
    return pl.pallas_call(
        grid_kernel,
        out_shape=jax.ShapeDtypeStruct((NT, SIDE, 2 * SIDE), f32),
        in_specs=[VMEM] * 3 + [SMEM] * 6 + [VMEM],
        out_specs=VMEM,
        scratch_shapes=[
            pltpu.VMEM((NT, 2 * SIDE, 2 * SIDE), bf16),
            pltpu.VMEM((NT, SIDE, 2 * SIDE), f32),
            pltpu.VMEM((NT, SIDE, 2 * SIDE), f32),
            pltpu.VMEM((G + 2 * PAD, 2 * SIDE), f32),
            pltpu.VMEM((SIDE, 2 * SIDE), f32),
            pltpu.VMEM((SIDE, 2 * SIDE), f32),
        ],
        compiler_params=pltpu.CompilerParams(vmem_limit_bytes=VMEM_LIMIT),
        name="grid_rows",
    )(model, observed, coords, count, block, cell, shift, tap_index, taps, jnp.asarray(row_tables()))


def imaged(columns, gain, offset, tap_index, taps):
    return pl.pallas_call(
        image_kernel,
        out_shape=jax.ShapeDtypeStruct((SIDE, G), f32),
        in_specs=[VMEM] * 2 + [SMEM] * 3 + [VMEM],
        out_specs=VMEM,
        scratch_shapes=[
            pltpu.VMEM((NT, SIDE, 2 * SIDE), f32),
            pltpu.VMEM((G + 2 * PAD, 2 * SIDE), f32),
            pltpu.VMEM((SIDE, G), f32),
        ],
        compiler_params=pltpu.CompilerParams(vmem_limit_bytes=VMEM_LIMIT),
        name="image_columns",
    )(columns, gain, offset, tap_index, taps, jnp.asarray(column_tables()))


def exchanged(blocks, n):
    return pl.pallas_call(
        functools.partial(exchange_kernel, n),
        out_shape=jax.ShapeDtypeStruct(blocks.shape, f32),
        in_specs=[VMEM],
        out_specs=VMEM,
        scratch_shapes=[
            pltpu.SemaphoreType.DMA((n,)),
            pltpu.SemaphoreType.DMA((n,)),
            pltpu.SemaphoreType.DMA,
        ],
        compiler_params=pltpu.CompilerParams(
            collective_id=0, has_side_effects=True, vmem_limit_bytes=VMEM_LIMIT
        ),
        name="exchange_tiles",
    )(blocks)


def local(
    model_grid, observed, coords, vis_count, subgrid_block, subgrid_cell, beam_gain,
    column_shift, row_offset, interp_index, interp_taps,
):
    blocks = gridded(
        model_grid, observed, coords, vis_count, subgrid_block, subgrid_cell,
        column_shift, interp_index, interp_taps,
    )
    columns = exchanged(blocks, NT)
    contribution = imaged(columns, beam_gain, row_offset, interp_index, interp_taps)
    tile_index = lax.axis_index("tile")
    upper = tile_index < column_shift[0]
    late = jnp.arange(G, dtype=jnp.int32) < row_offset[0]
    canvas = jnp.concatenate(
        [jnp.where(late, 0.0, contribution), jnp.where(late, contribution, 0.0)], axis=1
    )
    canvas = jnp.stack([jnp.where(upper, 0.0, canvas), jnp.where(upper, canvas, 0.0)])
    return lax.psum_scatter(canvas, "beam", scatter_dimension=2, tiled=True)


def solution(mesh):
    placed = (
        P("beam", None, "tile", None),
        P("beam", "tile", None, None),
        P("beam", "tile", None, None),
        P("beam", "tile", None),
        P("beam", "tile", None),
        P("beam", "tile", None),
        P("beam", "tile", None),
        P("beam"),
        P("beam"),
        P("beam", None),
        P(),
    )
    return jax.shard_map(
        local, mesh=mesh, in_specs=placed, out_specs=P(None, "tile", "beam"), check_vma=False
    )
```

profile of v0, /device:TPU:2, one launch (start us, length us, event | category | flops | bytes accessed | tf_op | source)
XLA Modules:
  0.0 115.9 jit_solution(17928362489670437005)
XLA Ops:
  6.5 0.0 reduce-scatter.2.cloned.1.call-start
  7.8 21.0 %grid_rows.1.blocks = f32[32,64,128]{2,1,0:T(8,128)} custom-call(f32[1,2,64,2048]{3,2,1,0:T(8,128)} %model.1, f32[1,64,2,256]{3,2,1,0:T(2,128)} %observed.1, f32[1,64,2,256]{3,2,1,0:T(2,128)} %coords.1, s32[1,1,64]{2,1,0:T(1,128)} %count.1, s32[1,1,64]{2,1,0:T(1,128)} %block.1, s32[1,1,64]{2,1,0:T(1,128)} %cell.1, s32[1]{0:T(128)} %copy.14.shift, ...), custom_call_target="tpu_custom_call" | custom-call | tf_op jit(solution)/shard_map/grid_rows/pallas_call | solution.py:250
  28.9 23.4 %exchange_tiles.1.columns = f32[32,64,128]{2,1,0:T(8,128)} custom-call(f32[32,64,128]{2,1,0:T(8,128)} %grid_rows.1.blocks), custom_call_target="tpu_custom_call" | custom-call | tf_op jit(solution)/shard_map/exchange_tiles/pallas_call | solution.py:285
  52.3 6.9 %image_columns.1 = f32[64,2048]{1,0:T(8,128)} custom-call(f32[32,64,128]{2,1,0:T(8,128)} %exchange_tiles.1.columns, f32[1,64,2048]{2,1,0:T(8,128)} %gain.1, s32[1]{0:T(128)} %copy.15.offset, s32[1,2]{1,0:T(1,128)} %tap_index.3, f32[8,5]{1,0:T(8,128)} %taps.3, bf16[32,128,256]{2,1,0:T(8,128)(2,1)} %constant.11.clone.table), custom_call_target="tpu_custom_call" | custom-call | tf_op jit(solution)/shard_map/image_columns/pallas_call | solution.py:269
  59.2 1.1 select_bitcast_fusion.1
  60.3 0.2 fusion.1
  60.6 1.5 %pad_maximum_fusion = f32[2,64,4096]{2,1,0:T(8,128)} fusion(f32[1,64,4096]{2,1,0:T(8,128)S(1)} %get-tuple-element.6, f32[1,64,4096]{2,1,0:T(8,128)S(1)} %get-tuple-element.5), kind=kLoop, calls=%fused_computation | loop fusion | flops 524288 | bytes 4194304 | tf_op jit(solution)/shard_map/stack | solution.py:318
  62.1 0.0 reduce-scatter.2.cloned.1.call-update
  62.1 47.0 %reduce-scatter.2.cloned.1.call-done = f32[2,64,512]{2,1,0:T(8,128)} async-done(((f32[2,64,4096]{2,1,0:T(8,128)}), f32[2,64,512]{2,1,0:T(8,128)}) %reduce-scatter.2.cloned.1.call-update) | async-done | bytes 262160 | tf_op jit(solution)/shard_map/reduce_scatter | solution.py:319
  (1 shorter events, 0.0 us)
Async XLA Ops:
  6.5 102.6 %reduce-scatter.2.cloned.1.call-start = ((), (), s32[]{:S(2)}) async-start(), calls=%async_computation.1 | async-start | bytes 2359296 | tf_op jit(solution)/shard_map/reduce_scatter | solution.py:319
Sparse Core Ops, SparseCore 0:
  62.2 46.8 reduce-scatter.1
where the time goes:
time: 117 us; the launch traced here: 116 us
  Pallas kernels  51.3 us (44%)
  waiting for transfers between devices  47 us (40%)
  between operations  14.7 us (13%)
  other arithmetic  2.86 us (2%)
    reduce_scatter x1, waiting for transfers between devices, local(): return lax.psum_scatter(canvas, 'beam', scatter_dimension=2, tiled=True)  47 us
    pallas_call x1, Pallas kernels, exchanged(): pl.pallas_call(functools.partial(exchange_kernel, n), out_shape=jax.Shape...  23.4 us
    pallas_call x1, Pallas kernels, gridded(): pl.pallas_call(grid_kernel, out_shape=jax.ShapeDtypeStruct((NT, SIDE, 2 *...  21 us
    pallas_call x1, Pallas kernels, imaged(): pl.pallas_call(image_kernel, out_shape=jax.ShapeDtypeStruct((SIDE, G), f3...  6.93 us
  transfers between devices with their start and end apart: 1, of which 1 were waited for; matrix products, arithmetic and copies ran while one was open for 0% of the time, Pallas kernels for 0%

commit v1 on v0

--- a/solution.py
+++ b/solution.py
@@ -16,6 +16,8 @@
 SUBS = 64
 SCALE = 3.0
 PAD = 8
+CHUNK = 512
+META = 8
 VMEM_LIMIT = 56 * 1024 * 1024
 MESH = pl.DeviceIdType.MESH
 
@@ -186,7 +188,9 @@
     lax.fori_loop(0, NT, send_block, 0)
 
 
-def image_kernel(columns, gain, offset, tap_index, taps, table, out, spectrum, padded, smooth):
+def image_kernel(
+    columns, gain, offset, shift, tap_index, taps, table, out, spectrum, padded, smooth
+):
     transform_leading(columns, spectrum)
     zeros = jnp.zeros((PAD, SIDE), f32)
     padded[pl.ds(0, PAD), pl.ds(0, SIDE)] = zeros
@@ -210,7 +214,14 @@
         turned = total.T[:SIDE]
         at = pl.ds(part * 128, 128)
         smooth[:, at] = turned * gain[0, :, at]
-    out[...] = pltpu.roll(smooth[...], offset[0], 1)
+    rolled = pltpu.roll(smooth[...], offset[0], 1)
+    upper = jnp.where(lax.axis_index("tile") < shift[0], 1.0, 0.0)
+    first = jnp.full((META, CHUNK), offset[0].astype(f32))
+    kind = lax.broadcasted_iota(jnp.int32, (META, CHUNK), 0)
+    facts = jnp.where(kind == 0, first, upper)
+    for chunk in range(4):
+        out[chunk % 2, chunk // 2, pl.ds(0, SIDE), :] = rolled[:, chunk * CHUNK : (chunk + 1) * CHUNK]
+        out[chunk % 2, chunk // 2, pl.ds(SIDE, META), :] = facts
 
 
 def exchange_kernel(n, blocks, out, send_sem, recv_sem, own_sem):
@@ -239,6 +250,76 @@
     own.wait()
     for copy in copies:
         copy.wait()
+
+
+def sum_kernel(pieces, out, paired, terms, landed, send_sem, recv_sem):
+    beam = lax.axis_index("beam")
+    level, core = beam // 2, lax.rem(beam, 2)
+    mate = beam + 1 - 2 * core
+    up, down = lax.rem(beam + 2, 8), lax.rem(beam + 6, 8)
+    barrier = pltpu.get_barrier_semaphore()
+    for peer in (mate, up, down):
+        pl.semaphore_signal(barrier, inc=1, device_id={"beam": peer}, device_id_type=MESH)
+    pl.semaphore_wait(barrier, 3)
+
+    def send(number, source, target, peer):
+        copy = pltpu.make_async_remote_copy(
+            src_ref=source,
+            dst_ref=target,
+            send_sem=send_sem.at[number],
+            recv_sem=recv_sem.at[number],
+            device_id={"beam": peer},
+            device_id_type=MESH,
+        )
+        copy.start()
+        return copy
+
+    pair = send(0, pieces.at[1 - core], paired, mate)
+    lane = lax.broadcasted_iota(jnp.int32, (1, CHUNK), 1)
+
+    def term(source, half, which):
+        part, late = lax.rem(half, 2), half // 2
+        row = (lane + CHUNK * (2 * part + core)).astype(f32)
+        facts = source[part, pl.ds(SIDE, META), :]
+        is_late = jnp.where(row < facts[0:1], 1, 0)
+        here = (is_late == late) & (facts[1:2] == float(which))
+        return jnp.where(here, source[part, pl.ds(0, SIDE), :], 0.0)
+
+    own = pieces.at[core]
+    pair.wait_recv()
+
+    def both(half, which):
+        return term(own, half, which) + term(paired, half, which)
+
+    far, above, below = lax.rem(level + 2, 4), lax.rem(level + 1, 4), lax.rem(level + 3, 4)
+    terms[0] = both(far, 0)
+    far_up = send(1, terms.at[0], landed.at[0], up)
+    terms[1] = both(far, 1)
+    far_down = send(2, terms.at[1], landed.at[1], down)
+    terms[2] = both(above, 1)
+    near_up = send(3, terms.at[2], landed.at[2], up)
+    terms[3] = both(below, 0)
+    near_down = send(4, terms.at[3], landed.at[3], down)
+    terms[4] = both(above, 0)
+    terms[5] = both(below, 1)
+    far_up.wait_recv()
+    terms[4] += landed[0]
+    last_up = send(5, terms.at[4], landed.at[4], up)
+    far_down.wait_recv()
+    terms[5] += landed[1]
+    last_down = send(6, terms.at[5], landed.at[5], down)
+    out[0] = both(level, 0)
+    out[1] = both(level, 1)
+    near_up.wait_recv()
+    out[1] += landed[2]
+    near_down.wait_recv()
+    out[0] += landed[3]
+    last_up.wait_recv()
+    out[0] += landed[4]
+    last_down.wait_recv()
+    out[1] += landed[5]
+    for copy in (pair, far_up, far_down, near_up, near_down, last_up, last_down):
+        copy.wait_send()
 
 
 SMEM = pl.BlockSpec(memory_space=pltpu.SMEM)
@@ -265,11 +346,11 @@
     )(model, observed, coords, count, block, cell, shift, tap_index, taps, jnp.asarray(row_tables()))
 
 
-def imaged(columns, gain, offset, tap_index, taps):
+def imaged(columns, gain, offset, shift, tap_index, taps):
     return pl.pallas_call(
         image_kernel,
-        out_shape=jax.ShapeDtypeStruct((SIDE, G), f32),
-        in_specs=[VMEM] * 2 + [SMEM] * 3 + [VMEM],
+        out_shape=jax.ShapeDtypeStruct((2, 2, SIDE + META, CHUNK), f32),
+        in_specs=[VMEM] * 2 + [SMEM] * 4 + [VMEM],
         out_specs=VMEM,
         scratch_shapes=[
             pltpu.VMEM((NT, SIDE, 2 * SIDE), f32),
@@ -278,7 +359,7 @@
         ],
         compiler_params=pltpu.CompilerParams(vmem_limit_bytes=VMEM_LIMIT),
         name="image_columns",
-    )(columns, gain, offset, tap_index, taps, jnp.asarray(column_tables()))
+    )(columns, gain, offset, shift, tap_index, taps, jnp.asarray(column_tables()))
 
 
 def exchanged(blocks, n):
@@ -299,6 +380,26 @@
     )(blocks)
 
 
+def summed(pieces):
+    return pl.pallas_call(
+        sum_kernel,
+        out_shape=jax.ShapeDtypeStruct((2, SIDE, CHUNK), f32),
+        in_specs=[VMEM],
+        out_specs=VMEM,
+        scratch_shapes=[
+            pltpu.VMEM((2, SIDE + META, CHUNK), f32),
+            pltpu.VMEM((6, SIDE, CHUNK), f32),
+            pltpu.VMEM((6, SIDE, CHUNK), f32),
+            pltpu.SemaphoreType.DMA((7,)),
+            pltpu.SemaphoreType.DMA((7,)),
+        ],
+        compiler_params=pltpu.CompilerParams(
+            collective_id=1, has_side_effects=True, vmem_limit_bytes=VMEM_LIMIT
+        ),
+        name="sum_beams",
+    )(pieces)
+
+
 def local(
     model_grid, observed, coords, vis_count, subgrid_block, subgrid_cell, beam_gain,
     column_shift, row_offset, interp_index, interp_taps,
@@ -308,15 +409,8 @@
         column_shift, interp_index, interp_taps,
     )
     columns = exchanged(blocks, NT)
-    contribution = imaged(columns, beam_gain, row_offset, interp_index, interp_taps)
-    tile_index = lax.axis_index("tile")
-    upper = tile_index < column_shift[0]
-    late = jnp.arange(G, dtype=jnp.int32) < row_offset[0]
-    canvas = jnp.concatenate(
-        [jnp.where(late, 0.0, contribution), jnp.where(late, contribution, 0.0)], axis=1
-    )
-    canvas = jnp.stack([jnp.where(upper, 0.0, canvas), jnp.where(upper, canvas, 0.0)])
-    return lax.psum_scatter(canvas, "beam", scatter_dimension=2, tiled=True)
+    pieces = imaged(columns, beam_gain, row_offset, column_shift, interp_index, interp_taps)
+    return summed(pieces)
 
 
 def solution(mesh):

time: 117 us -> 83.4 us (0.71)
  the two profiles are of different devices: /device:TPU:2 before, /device:TPU:31 now
where the time goes in v1:
time: 83.4 us; the launch traced here: 83.1 us
  Pallas kernels  80.1 us (96%)
  local copies, waits for them, and re-layouts  1.67 us (2%)
  between operations  1.32 us (2%)
    pallas_call x1, Pallas kernels, summed(): pl.pallas_call(sum_kernel, out_shape=jax.ShapeDtypeStruct((2, SIDE, CHUNK...  29.4 us
    pallas_call x1, Pallas kernels, exchanged(): pl.pallas_call(functools.partial(exchange_kernel, n), out_shape=jax.Shape...  22.7 us
    pallas_call x1, Pallas kernels, gridded(): pl.pallas_call(grid_kernel, out_shape=jax.ShapeDtypeStruct((NT, SIDE, 2 *...  21 us
    pallas_call x1, Pallas kernels, imaged(): pl.pallas_call(image_kernel, out_shape=jax.ShapeDtypeStruct((2, 2, SIDE +...  6.96 us
    unnamed x1, local copies, waits for them, and re-layouts  1.67 us

profile of v1, /device:TPU:31, one launch (start us, length us, event | category | flops | bytes accessed | tf_op | source)
XLA Modules:
  0.0 83.1 jit_solution(12669642287297065215)
XLA Ops:
  0.7 21.0 %grid_rows.1.blocks = f32[32,64,128]{2,1,0:T(8,128)} custom-call(f32[1,2,64,2048]{3,2,1,0:T(8,128)} %model.1, f32[1,64,2,256]{3,2,1,0:T(2,128)} %observed.1, f32[1,64,2,256]{3,2,1,0:T(2,128)} %coords.1, s32[1,1,64]{2,1,0:T(1,128)} %count.1, s32[1,1,64]{2,1,0:T(1,128)} %block.1, s32[1,1,64]{2,1,0:T(1,128)} %cell.1, s32[1]{0:T(128)S(6)} %copy.15.shift, ...), custom_call_target="tpu_custom_call" | custom-call | tf_op jit(solution)/shard_map/grid_rows/pallas_call | solution.py:331
  21.7 22.7 %exchange_tiles.1.columns = f32[32,64,128]{2,1,0:T(8,128)} custom-call(f32[32,64,128]{2,1,0:T(8,128)} %grid_rows.1.blocks), custom_call_target="tpu_custom_call" | custom-call | tf_op jit(solution)/shard_map/exchange_tiles/pallas_call | solution.py:366
  45.0 7.0 %image_columns.1.pieces = f32[2,2,72,512]{3,2,1,0:T(8,128)} custom-call(f32[32,64,128]{2,1,0:T(8,128)} %exchange_tiles.1.columns, f32[1,64,2048]{2,1,0:T(8,128)} %gain.1, s32[1]{0:T(128)S(6)} %copy.16.offset, s32[1]{0:T(128)S(6)} %copy.15.shift, s32[1,2]{1,0:T(1,128)} %tap_index.3, f32[8,5]{1,0:T(8,128)} %taps.3, bf16[32,128,256]{2,1,0:T(8,128)(2,1)} %constant.5.clone.table), custom_call_target="tpu_custom_call" | custom-call | tf_op jit(solution)/shard_map/image_columns/pallas_call | solution.py:350
  52.0 29.4 %sum_beams.1 = f32[2,64,512]{2,1,0:T(8,128)} custom-call(f32[2,2,72,512]{3,2,1,0:T(8,128)} %image_columns.1.pieces), custom_call_target="tpu_custom_call" | custom-call | tf_op jit(solution)/shard_map/sum_beams/pallas_call | solution.py:384
  81.5 1.7 %copy.17 = f32[2,64,512]{2,1,0:T(8,128)} copy(f32[2,64,512]{2,1,0:T(8,128)} %sum_beams.1) | data formatting | bytes 524288

commit v2 on v0

--- a/solution.py
+++ b/solution.py
@@ -1,4 +1,3 @@
-import functools
 import math
 
 import jax
@@ -16,6 +15,11 @@
 SUBS = 64
 SCALE = 3.0
 PAD = 8
+BEAMS = 8
+CHUNK = 512
+GROUPS = 4
+ROWS = SIDE // GROUPS
+META = 8
 VMEM_LIMIT = 56 * 1024 * 1024
 MESH = pl.DeviceIdType.MESH
 
@@ -186,59 +190,174 @@
     lax.fori_loop(0, NT, send_block, 0)
 
 
-def image_kernel(columns, gain, offset, tap_index, taps, table, out, spectrum, padded, smooth):
-    transform_leading(columns, spectrum)
-    zeros = jnp.zeros((PAD, SIDE), f32)
-    padded[pl.ds(0, PAD), pl.ds(0, SIDE)] = zeros
-    padded[pl.ds(PAD + G, PAD), pl.ds(0, SIDE)] = zeros
-    for y1 in range(NT):
-        high, low = split(spectrum[y1])
-        both = lax.dot_general(
-            table[y1],
-            jnp.concatenate([high, low], axis=1),
-            (((1,), (1,)), ((), ())),
-            preferred_element_type=f32,
-        )
-        padded[pl.ds(PAD + y1, SIDE, stride=NT), pl.ds(0, SIDE)] = both[:SIDE] + both[SIDE:]
+def tail_kernel(
+    blocks, gain, offset, shift, tap_index, taps, table, out,
+    landing, spectrum, padded, smooth, pieces, paired, terms, landed,
+    own_sem, tile_send, tile_recv, pair_send, pair_recv, ring_send, ring_recv,
+):
+    me = lax.axis_index("tile")
+    beam = lax.axis_index("beam")
+    level, core = beam // 2, lax.rem(beam, 2)
+    mate = beam + 1 - 2 * core
+    up, down = lax.rem(beam + 2, BEAMS), lax.rem(beam + 6, BEAMS)
+    barrier = pltpu.get_barrier_semaphore()
+    for step in range(1, NT):
+        pl.semaphore_signal(
+            barrier, inc=1, device_id={"tile": lax.rem(me + step, NT)}, device_id_type=MESH
+        )
+    for peer in (mate, up, down):
+        pl.semaphore_signal(barrier, inc=1, device_id={"beam": peer}, device_id_type=MESH)
+    own = pltpu.make_async_copy(blocks.at[me], landing.at[me], own_sem)
+    own.start()
+    padded[pl.ds(0, PAD), :] = jnp.zeros((PAD, 2 * SIDE), f32)
+    padded[pl.ds(PAD + G, PAD), :] = jnp.zeros((PAD, 2 * SIDE), f32)
+    pl.semaphore_wait(barrier, NT + 2)
+
+    def rows_of(g):
+        return pl.ds(pl.multiple_of(g * ROWS, ROWS), ROWS)
+
+    def send_group(g, carry):
+        def send_one(step, inner):
+            peer = lax.rem(me + step, NT)
+            pltpu.make_async_remote_copy(
+                src_ref=blocks.at[peer, rows_of(g)],
+                dst_ref=landing.at[me, rows_of(g)],
+                send_sem=tile_send.at[g],
+                recv_sem=tile_recv.at[g],
+                device_id={"tile": peer},
+                device_id_type=MESH,
+            ).start()
+            return inner
+
+        return lax.fori_loop(1, NT, send_one, carry)
+
+    lax.fori_loop(0, GROUPS, send_group, 0)
+    own.wait()
+
+    def wait_group(g, semaphores):
+        most = pl.ds(0, NT - 1)
+        pltpu.make_async_copy(
+            blocks.at[most, rows_of(g)], landing.at[most, rows_of(g)], semaphores.at[g]
+        ).wait()
 
     phase = tap_index[0, 1]
     weights = [taps[phase, tap] for tap in range(5)]
-    for part in range(G // 128):
-        total = weights[0] * padded[pl.ds(part * 128 + PAD + 2, 128), :]
-        for tap in range(1, 5):
-            total = total + weights[tap] * padded[pl.ds(part * 128 + PAD + 2 - tap, 128), :]
-        turned = total.T[:SIDE]
-        at = pl.ds(part * 128, 128)
-        smooth[:, at] = turned * gain[0, :, at]
-    out[...] = pltpu.roll(smooth[...], offset[0], 1)
-
-
-def exchange_kernel(n, blocks, out, send_sem, recv_sem, own_sem):
-    me = lax.axis_index("tile")
-    barrier = pltpu.get_barrier_semaphore()
-    for step in range(1, n):
-        pl.semaphore_signal(
-            barrier, inc=1, device_id={"tile": lax.rem(me + step, n)}, device_id_type=MESH
-        )
-    own = pltpu.make_async_copy(blocks.at[me], out.at[me], own_sem)
-    own.start()
-    pl.semaphore_wait(barrier, n - 1)
-    copies = []
-    for step in range(1, n):
-        peer = lax.rem(me + step, n)
-        copy = pltpu.make_async_remote_copy(
-            src_ref=blocks.at[peer],
-            dst_ref=out.at[me],
-            send_sem=send_sem.at[step],
-            recv_sem=recv_sem.at[step],
-            device_id={"tile": peer},
+    signs = lane_signs((8, 2 * SIDE))
+    upper = jnp.where(me < shift[0], 1.0, 0.0)
+    first = jnp.full((META, CHUNK), offset[0].astype(f32))
+    kind = lax.broadcasted_iota(jnp.int32, (META, CHUNK), 0)
+    facts = jnp.where(kind == 0, first, upper)
+
+    def image_group(g):
+        def tile(i, carry):
+            start = pl.multiple_of(g * ROWS + i * 8, 8)
+            values = transform([landing[t, pl.ds(start, 8), :] for t in range(NT)], signs)
+            at = pl.ds(pl.multiple_of(i * 8, 8), 8)
+            for y1, value in enumerate(values):
+                spectrum[y1, at, :] = value
+            return carry
+
+        lax.fori_loop(0, ROWS // 8, tile, 0)
+        for y1 in range(NT):
+            high, low = split(spectrum[y1])
+            both = lax.dot_general(
+                table[y1],
+                jnp.concatenate([high, low], axis=1),
+                (((1,), (1,)), ((), ())),
+                preferred_element_type=f32,
+            )
+            padded[pl.ds(PAD + y1, SIDE, stride=NT), pl.ds(0, ROWS)] = both[:SIDE] + both[SIDE:]
+        for part in range(G // 128):
+            total = weights[0] * padded[pl.ds(part * 128 + PAD + 2, 128), :]
+            for tap in range(1, 5):
+                total = total + weights[tap] * padded[pl.ds(part * 128 + PAD + 2 - tap, 128), :]
+            at = pl.ds(part * 128, 128)
+            smooth[:, at] = total.T[:ROWS] * gain[0, rows_of(g), at]
+        rolled = pltpu.roll(smooth[...], offset[0], 1)
+        for chunk in range(4):
+            piece = rolled[:, chunk * CHUNK : (chunk + 1) * CHUNK]
+            pieces[g, chunk % 2, chunk // 2, pl.ds(0, ROWS), :] = piece
+            pieces[g, chunk % 2, chunk // 2, pl.ds(ROWS, META), :] = facts
+
+    def pair(g):
+        return pltpu.make_async_remote_copy(
+            src_ref=pieces.at[g, 1 - core],
+            dst_ref=paired.at[g],
+            send_sem=pair_send.at[g],
+            recv_sem=pair_recv.at[g],
+            device_id={"beam": mate},
             device_id_type=MESH,
         )
-        copy.start()
-        copies.append(copy)
-    own.wait()
-    for copy in copies:
-        copy.wait()
+
+    def ring(g, number, peer):
+        return pltpu.make_async_remote_copy(
+            src_ref=terms.at[g, number],
+            dst_ref=landed.at[g, number],
+            send_sem=ring_send.at[g, number],
+            recv_sem=ring_recv.at[g, number],
+            device_id={"beam": peer},
+            device_id_type=MESH,
+        )
+
+    lane = lax.broadcasted_iota(jnp.int32, (1, CHUNK), 1)
+
+    def term(source, half, which):
+        part, late = lax.rem(half, 2), half // 2
+        row = (lane + CHUNK * (2 * part + core)).astype(f32)
+        told = source[part, pl.ds(ROWS, META), :]
+        is_late = jnp.where(row < told[0:1], 1, 0)
+        here = (is_late == late) & (told[1:2] == float(which))
+        return jnp.where(here, source[part, pl.ds(0, ROWS), :], 0.0)
+
+    def both_terms(g, half, which):
+        return term(pieces.at[g, core], half, which) + term(paired.at[g], half, which)
+
+    far, above, below = lax.rem(level + 2, 4), lax.rem(level + 1, 4), lax.rem(level + 3, 4)
+    peers = (up, down, up, down, up, down)
+
+    def first_hop(g):
+        pair(g).wait_recv()
+        for number, half, which in ((0, far, 0), (1, far, 1), (2, above, 1), (3, below, 0)):
+            terms[g, number] = both_terms(g, half, which)
+            ring(g, number, peers[number]).start()
+        terms[g, 4] = both_terms(g, above, 0)
+        terms[g, 5] = both_terms(g, below, 1)
+
+    def second_hop(g):
+        for number in (0, 1):
+            ring(g, number, peers[number]).wait_recv()
+            terms[g, 4 + number] += landed[g, number]
+            ring(g, 4 + number, peers[4 + number]).start()
+
+    def group(g, carry):
+        wait_group(g, tile_recv)
+        image_group(g)
+        pair(g).start()
+
+        @pl.when(g > 0)
+        def _():
+            second_hop(g - 1)
+
+        first_hop(g)
+        return carry
+
+    lax.fori_loop(0, GROUPS, group, 0)
+    second_hop(GROUPS - 1)
+
+    def finish(g, carry):
+        wait_group(g, tile_send)
+        pair(g).wait_send()
+        for which in (0, 1):
+            total = both_terms(g, level, which)
+            for number in (3 - which, 4 + which):
+                ring(g, number, peers[number]).wait_recv()
+                total += landed[g, number]
+            out[which, rows_of(g), :] = total
+        for number in range(6):
+            ring(g, number, peers[number]).wait_send()
+        return carry
+
+    lax.fori_loop(0, GROUPS, finish, 0)
 
 
 SMEM = pl.BlockSpec(memory_space=pltpu.SMEM)
@@ -265,38 +384,34 @@
     )(model, observed, coords, count, block, cell, shift, tap_index, taps, jnp.asarray(row_tables()))
 
 
-def imaged(columns, gain, offset, tap_index, taps):
+def finished(blocks, gain, offset, shift, tap_index, taps):
     return pl.pallas_call(
-        image_kernel,
-        out_shape=jax.ShapeDtypeStruct((SIDE, G), f32),
-        in_specs=[VMEM] * 2 + [SMEM] * 3 + [VMEM],
+        tail_kernel,
+        out_shape=jax.ShapeDtypeStruct((2, SIDE, CHUNK), f32),
+        in_specs=[VMEM] * 2 + [SMEM] * 4 + [VMEM],
         out_specs=VMEM,
         scratch_shapes=[
             pltpu.VMEM((NT, SIDE, 2 * SIDE), f32),
+            pltpu.VMEM((NT, ROWS, 2 * SIDE), f32),
             pltpu.VMEM((G + 2 * PAD, 2 * SIDE), f32),
-            pltpu.VMEM((SIDE, G), f32),
-        ],
-        compiler_params=pltpu.CompilerParams(vmem_limit_bytes=VMEM_LIMIT),
-        name="image_columns",
-    )(columns, gain, offset, tap_index, taps, jnp.asarray(column_tables()))
-
-
-def exchanged(blocks, n):
-    return pl.pallas_call(
-        functools.partial(exchange_kernel, n),
-        out_shape=jax.ShapeDtypeStruct(blocks.shape, f32),
-        in_specs=[VMEM],
-        out_specs=VMEM,
-        scratch_shapes=[
-            pltpu.SemaphoreType.DMA((n,)),
-            pltpu.SemaphoreType.DMA((n,)),
+            pltpu.VMEM((ROWS, G), f32),
+            pltpu.VMEM((GROUPS, 2, 2, ROWS + META, CHUNK), f32),
+            pltpu.VMEM((GROUPS, 2, ROWS + META, CHUNK), f32),
+            pltpu.VMEM((GROUPS, 6, ROWS, CHUNK), f32),
+            pltpu.VMEM((GROUPS, 6, ROWS, CHUNK), f32),
             pltpu.SemaphoreType.DMA,
+            pltpu.SemaphoreType.DMA((GROUPS,)),
+            pltpu.SemaphoreType.DMA((GROUPS,)),
+            pltpu.SemaphoreType.DMA((GROUPS,)),
+            pltpu.SemaphoreType.DMA((GROUPS,)),
+            pltpu.SemaphoreType.DMA((GROUPS, 6)),
+            pltpu.SemaphoreType.DMA((GROUPS, 6)),
         ],
         compiler_params=pltpu.CompilerParams(
             collective_id=0, has_side_effects=True, vmem_limit_bytes=VMEM_LIMIT
         ),
-        name="exchange_tiles",
-    )(blocks)
+        name="image_and_sum",
+    )(blocks, gain, offset, shift, tap_index, taps, jnp.asarray(column_tables()))
 
 
 def local(
@@ -307,16 +422,7 @@
         model_grid, observed, coords, vis_count, subgrid_block, subgrid_cell,
         column_shift, interp_index, interp_taps,
     )
-    columns = exchanged(blocks, NT)
-    contribution = imaged(columns, beam_gain, row_offset, interp_index, interp_taps)
-    tile_index = lax.axis_index("tile")
-    upper = tile_index < column_shift[0]
-    late = jnp.arange(G, dtype=jnp.int32) < row_offset[0]
-    canvas = jnp.concatenate(
-        [jnp.where(late, 0.0, contribution), jnp.where(late, contribution, 0.0)], axis=1
-    )
-    canvas = jnp.stack([jnp.where(upper, 0.0, canvas), jnp.where(upper, canvas, 0.0)])
-    return lax.psum_scatter(canvas, "beam", scatter_dimension=2, tiled=True)
+    return finished(blocks, beam_gain, row_offset, column_shift, interp_index, interp_taps)
 
 
 def solution(mesh):

time: 117 us -> 74.4 us (0.64)
  the two profiles are of different devices: /device:TPU:2 before, /device:TPU:14 now
where the time goes in v2:
time: 74.4 us; the launch traced here: 74.3 us
  Pallas kernels  71.3 us (96%)
  local copies, waits for them, and re-layouts  1.67 us (2%)
  between operations  1.31 us (2%)
    pallas_call x1, Pallas kernels, finished(): pl.pallas_call(tail_kernel, out_shape=jax.ShapeDtypeStruct((2, SIDE, CHUN...  50.3 us
    pallas_call x1, Pallas kernels, gridded(): pl.pallas_call(grid_kernel, out_shape=jax.ShapeDtypeStruct((NT, SIDE, 2 *...  21 us
    unnamed x1, local copies, waits for them, and re-layouts  1.67 us

profile of v2, /device:TPU:14, one launch (start us, length us, event | category | flops | bytes accessed | tf_op | source)
XLA Modules:
  0.0 74.3 jit_solution(16386688009868255518)
XLA Ops:
  1.3 21.0 %grid_rows.1.blocks = f32[32,64,128]{2,1,0:T(8,128)} custom-call(f32[1,2,64,2048]{3,2,1,0:T(8,128)} %model.1, f32[1,64,2,256]{3,2,1,0:T(2,128)} %observed.1, f32[1,64,2,256]{3,2,1,0:T(2,128)} %coords.1, s32[1,1,64]{2,1,0:T(1,128)} %count.1, s32[1,1,64]{2,1,0:T(1,128)} %block.1, s32[1,1,64]{2,1,0:T(1,128)} %cell.1, s32[1]{0:T(128)S(6)} %copy.15.shift, ...), custom_call_target="tpu_custom_call" | custom-call | tf_op jit(solution)/shard_map/grid_rows/pallas_call | solution.py:369
  22.3 50.3 %image_and_sum.1 = f32[2,64,512]{2,1,0:T(8,128)} custom-call(f32[32,64,128]{2,1,0:T(8,128)} %grid_rows.1.blocks, f32[1,64,2048]{2,1,0:T(8,128)} %gain.1, s32[1]{0:T(128)S(6)} %copy.16.offset, s32[1]{0:T(128)S(6)} %copy.15.shift, s32[1,2]{1,0:T(1,128)} %tap_index.3, f32[8,5]{1,0:T(8,128)} %taps.3, bf16[32,128,256]{2,1,0:T(8,128)(2,1)} %constant.5.clone.table), custom_call_target="tpu_custom_call" | custom-call | tf_op jit(solution)/shard_map/image_and_sum/pallas_call | solution.py:388
  72.6 1.7 %copy.17 = f32[2,64,512]{2,1,0:T(8,128)} copy(f32[2,64,512]{2,1,0:T(8,128)} %image_and_sum.1) | data formatting | bytes 524288

commit v3 on v2

--- a/solution.py
+++ b/solution.py
@@ -88,21 +88,8 @@
     return low + high
 
 
-def transform_leading(source, target):
-    signs = lane_signs((8, 2 * SIDE))
-
-    def tile(i, carry):
-        at = pl.ds(pl.multiple_of(i * 8, 8), 8)
-        for k, value in enumerate(transform([source[q, at, :] for q in range(NT)], signs)):
-            target[k, at, :] = value
-        return carry
-
-    lax.fori_loop(0, SIDE // 8, tile, 0)
-
-
 def grid_kernel(
-    model, observed, coords, count, block, cell, shift, tap_index, taps, table, out,
-    windows, grid, spectrum, padded, rising, falling,
+    model, observed, coords, count, block, cell, grid, windows, rising, falling
 ):
     row = lax.broadcasted_iota(jnp.int32, (SIDE, 2 * SIDE), 0).astype(f32)
     rising[...] = jnp.exp(row / SCALE)
@@ -164,36 +151,12 @@
 
     lax.fori_loop(0, SUBS // 4, several, 0)
 
-    transform_leading(grid, spectrum)
-    signs = lane_signs((SIDE, 2 * SIDE))
-    padded[pl.ds(0, PAD), :] = jnp.zeros((PAD, 2 * SIDE), f32)
-    padded[pl.ds(PAD + G, PAD), :] = jnp.zeros((PAD, 2 * SIDE), f32)
-    for x1 in range(NT):
-        high, low = split(spectrum[x1])
-        both = jnp.dot(
-            table[x1], jnp.concatenate([high, low, high], axis=0), preferred_element_type=f32
-        )
-        padded[pl.ds(PAD + x1, SIDE, stride=NT), :] = both[:SIDE] + swapped(both[SIDE:]) * signs
-
-    phase = tap_index[0, 0]
-    weights = [taps[phase, tap] for tap in range(5)]
-    steps = shift[0]
-
-    def send_block(d, carry):
-        start = pl.multiple_of(d * SIDE, SIDE)
-        total = weights[0] * padded[pl.ds(start + PAD + 2, SIDE), :]
-        for tap in range(1, 5):
-            total = total + weights[tap] * padded[pl.ds(start + PAD + 2 - tap, SIDE), :]
-        out[(d + steps) % NT] = total
-        return carry
-
-    lax.fori_loop(0, NT, send_block, 0)
-
 
 def tail_kernel(
-    blocks, gain, offset, shift, tap_index, taps, table, out,
-    landing, spectrum, padded, smooth, pieces, paired, terms, landed,
-    own_sem, tile_send, tile_recv, pair_send, pair_recv, ring_send, ring_recv,
+    grid, gain_in, offset, shift, tap_index, taps, row_table_in, table_in, out,
+    row_table, table, gain, tapped, blocks, landing, spectrum, padded, smooth,
+    pieces, paired, terms, landed,
+    in_sem, tile_send, tile_recv, pair_send, pair_recv, ring_send, ring_recv,
 ):
     me = lax.axis_index("tile")
     beam = lax.axis_index("beam")
@@ -207,16 +170,62 @@
         )
     for peer in (mate, up, down):
         pl.semaphore_signal(barrier, inc=1, device_id={"beam": peer}, device_id_type=MESH)
-    own = pltpu.make_async_copy(blocks.at[me], landing.at[me], own_sem)
-    own.start()
+    row_copy = pltpu.make_async_copy(row_table_in, row_table, in_sem.at[0])
+    row_copy.start()
+    column_copy = pltpu.make_async_copy(table_in, table, in_sem.at[1])
+    column_copy.start()
+    gain_copy = pltpu.make_async_copy(gain_in, gain, in_sem.at[2])
+    gain_copy.start()
+
+    signs = lane_signs((8, 2 * SIDE))
+
+    def transform_rows(source, start, rows):
+        def tile(i, carry):
+            at = pl.ds(pl.multiple_of(start + i * 8, 8), 8)
+            to = pl.ds(pl.multiple_of(i * 8, 8), 8)
+            for k, value in enumerate(transform([source[t, at, :] for t in range(NT)], signs)):
+                spectrum[k, to, :] = value
+            return carry
+
+        lax.fori_loop(0, rows // 8, tile, 0)
+
     padded[pl.ds(0, PAD), :] = jnp.zeros((PAD, 2 * SIDE), f32)
     padded[pl.ds(PAD + G, PAD), :] = jnp.zeros((PAD, 2 * SIDE), f32)
-    pl.semaphore_wait(barrier, NT + 2)
+    transform_rows(grid, 0, SIDE)
+    row_copy.wait()
+    wide_signs = lane_signs((SIDE, 2 * SIDE))
+    for x1 in range(NT):
+        high, low = split(spectrum[x1])
+        both = jnp.dot(
+            row_table[x1], jnp.concatenate([high, low, high], axis=0), preferred_element_type=f32
+        )
+        padded[pl.ds(PAD + x1, SIDE, stride=NT), :] = both[:SIDE] + swapped(both[SIDE:]) * wide_signs
 
     def rows_of(g):
         return pl.ds(pl.multiple_of(g * ROWS, ROWS), ROWS)
 
-    def send_group(g, carry):
+    phase_x = tap_index[0, 0]
+    weights_x = [taps[phase_x, tap] for tap in range(5)]
+    steps = shift[0]
+
+    def make_group(g):
+        def make(d, carry):
+            start = pl.multiple_of(d * SIDE + g * ROWS, ROWS)
+            total = weights_x[0] * padded[pl.ds(start + PAD + 2, ROWS), :]
+            for tap in range(1, 5):
+                total = total + weights_x[tap] * padded[pl.ds(start + PAD + 2 - tap, ROWS), :]
+            tapped[d] = total
+            return carry
+
+        def place(d, carry):
+            blocks[d, rows_of(g), :] = tapped[lax.rem(d - steps + NT, NT)]
+            return carry
+
+        lax.fori_loop(0, NT, make, 0)
+        lax.fori_loop(0, NT, place, 0)
+        landing[me, rows_of(g), :] = blocks[me, rows_of(g), :]
+
+    def send_group(g):
         def send_one(step, inner):
             peer = lax.rem(me + step, NT)
             pltpu.make_async_remote_copy(
@@ -229,10 +238,23 @@
             ).start()
             return inner
 
-        return lax.fori_loop(1, NT, send_one, carry)
-
-    lax.fori_loop(0, GROUPS, send_group, 0)
-    own.wait()
+        lax.fori_loop(1, NT, send_one, 0)
+
+    make_group(0)
+    pl.semaphore_wait(barrier, NT + 2)
+
+    def start_group(g, carry):
+        send_group(g)
+
+        @pl.when(g < GROUPS - 1)
+        def _():
+            make_group(g + 1)
+
+        return carry
+
+    lax.fori_loop(0, GROUPS, start_group, 0)
+    column_copy.wait()
+    gain_copy.wait()
 
     def wait_group(g, semaphores):
         most = pl.ds(0, NT - 1)
@@ -242,24 +264,15 @@
 
     phase = tap_index[0, 1]
     weights = [taps[phase, tap] for tap in range(5)]
-    signs = lane_signs((8, 2 * SIDE))
     upper = jnp.where(me < shift[0], 1.0, 0.0)
     first = jnp.full((META, CHUNK), offset[0].astype(f32))
     kind = lax.broadcasted_iota(jnp.int32, (META, CHUNK), 0)
     facts = jnp.where(kind == 0, first, upper)
 
     def image_group(g):
-        def tile(i, carry):
-            start = pl.multiple_of(g * ROWS + i * 8, 8)
-            values = transform([landing[t, pl.ds(start, 8), :] for t in range(NT)], signs)
-            at = pl.ds(pl.multiple_of(i * 8, 8), 8)
-            for y1, value in enumerate(values):
-                spectrum[y1, at, :] = value
-            return carry
-
-        lax.fori_loop(0, ROWS // 8, tile, 0)
+        transform_rows(landing, g * ROWS, ROWS)
         for y1 in range(NT):
-            high, low = split(spectrum[y1])
+            high, low = split(spectrum[y1, pl.ds(0, ROWS), :])
             both = lax.dot_general(
                 table[y1],
                 jnp.concatenate([high, low], axis=1),
@@ -336,12 +349,17 @@
 
         @pl.when(g > 0)
         def _():
-            second_hop(g - 1)
-
-        first_hop(g)
+            first_hop(g - 1)
+
+        @pl.when(g > 1)
+        def _():
+            second_hop(g - 2)
+
         return carry
 
     lax.fori_loop(0, GROUPS, group, 0)
+    first_hop(GROUPS - 1)
+    second_hop(GROUPS - 2)
     second_hop(GROUPS - 1)
 
     def finish(g, carry):
@@ -365,41 +383,43 @@
 ANY = pl.BlockSpec(memory_space=pl.ANY)
 
 
-def gridded(model, observed, coords, count, block, cell, shift, tap_index, taps):
+def gridded(model, observed, coords, count, block, cell):
     return pl.pallas_call(
         grid_kernel,
         out_shape=jax.ShapeDtypeStruct((NT, SIDE, 2 * SIDE), f32),
-        in_specs=[VMEM] * 3 + [SMEM] * 6 + [VMEM],
+        in_specs=[VMEM] * 3 + [SMEM] * 3,
         out_specs=VMEM,
         scratch_shapes=[
             pltpu.VMEM((NT, 2 * SIDE, 2 * SIDE), bf16),
-            pltpu.VMEM((NT, SIDE, 2 * SIDE), f32),
-            pltpu.VMEM((NT, SIDE, 2 * SIDE), f32),
-            pltpu.VMEM((G + 2 * PAD, 2 * SIDE), f32),
             pltpu.VMEM((SIDE, 2 * SIDE), f32),
             pltpu.VMEM((SIDE, 2 * SIDE), f32),
         ],
         compiler_params=pltpu.CompilerParams(vmem_limit_bytes=VMEM_LIMIT),
-        name="grid_rows",
-    )(model, observed, coords, count, block, cell, shift, tap_index, taps, jnp.asarray(row_tables()))
-
-
-def finished(blocks, gain, offset, shift, tap_index, taps):
+        name="grid_residuals",
+    )(model, observed, coords, count, block, cell)
+
+
+def finished(grid, gain, offset, shift, tap_index, taps):
     return pl.pallas_call(
         tail_kernel,
         out_shape=jax.ShapeDtypeStruct((2, SIDE, CHUNK), f32),
-        in_specs=[VMEM] * 2 + [SMEM] * 4 + [VMEM],
+        in_specs=[VMEM, ANY] + [SMEM] * 4 + [ANY] * 2,
         out_specs=VMEM,
         scratch_shapes=[
+            pltpu.VMEM((NT, 2 * SIDE, 3 * SIDE), bf16),
+            pltpu.VMEM((NT, 2 * SIDE, 4 * SIDE), bf16),
+            pltpu.VMEM((1, SIDE, G), f32),
+            pltpu.VMEM((NT, ROWS, 2 * SIDE), f32),
             pltpu.VMEM((NT, SIDE, 2 * SIDE), f32),
-            pltpu.VMEM((NT, ROWS, 2 * SIDE), f32),
+            pltpu.VMEM((NT, SIDE, 2 * SIDE), f32),
+            pltpu.VMEM((NT, SIDE, 2 * SIDE), f32),
             pltpu.VMEM((G + 2 * PAD, 2 * SIDE), f32),
             pltpu.VMEM((ROWS, G), f32),
             pltpu.VMEM((GROUPS, 2, 2, ROWS + META, CHUNK), f32),
             pltpu.VMEM((GROUPS, 2, ROWS + META, CHUNK), f32),
             pltpu.VMEM((GROUPS, 6, ROWS, CHUNK), f32),
             pltpu.VMEM((GROUPS, 6, ROWS, CHUNK), f32),
-            pltpu.SemaphoreType.DMA,
+            pltpu.SemaphoreType.DMA((3,)),
             pltpu.SemaphoreType.DMA((GROUPS,)),
             pltpu.SemaphoreType.DMA((GROUPS,)),
             pltpu.SemaphoreType.DMA((GROUPS,)),
@@ -411,18 +431,20 @@
             collective_id=0, has_side_effects=True, vmem_limit_bytes=VMEM_LIMIT
         ),
         name="image_and_sum",
-    )(blocks, gain, offset, shift, tap_index, taps, jnp.asarray(column_tables()))
+    )(
+        grid, gain, offset, shift, tap_index, taps,
+        jnp.asarray(row_tables()), jnp.asarray(column_tables()),
+    )
 
 
 def local(
     model_grid, observed, coords, vis_count, subgrid_block, subgrid_cell, beam_gain,
     column_shift, row_offset, interp_index, interp_taps,
 ):
-    blocks = gridded(
+    grid = gridded(
         model_grid, observed, coords, vis_count, subgrid_block, subgrid_cell,
-        column_shift, interp_index, interp_taps,
     )
-    return finished(blocks, beam_gain, row_offset, column_shift, interp_index, interp_taps)
+    return finished(grid, beam_gain, row_offset, column_shift, interp_index, interp_taps)
 
 
 def solution(mesh):

time: 74.4 us -> 65.6 us (0.88)
  the two profiles are of different devices: /device:TPU:14 before, /device:TPU:2 now
where the time goes in v3:
time: 65.6 us; the launch traced here: 65.2 us
  Pallas kernels  62.2 us (95%)
  local copies, waits for them, and re-layouts  1.67 us (3%)
  between operations  1.31 us (2%)
    pallas_call x1, Pallas kernels, finished(): pl.pallas_call(tail_kernel, out_shape=jax.ShapeDtypeStruct((2, SIDE, CHUN...  46.4 us
    pallas_call x1, Pallas kernels, gridded(): pl.pallas_call(grid_kernel, out_shape=jax.ShapeDtypeStruct((NT, SIDE, 2 *...  15.8 us
    unnamed x1, local copies, waits for them, and re-layouts  1.67 us

profile of v3, /device:TPU:2, one launch (start us, length us, event | category | flops | bytes accessed | tf_op | source)
XLA Modules:
  0.0 65.2 jit_solution(12477209809662736767)
XLA Ops:
  1.3 15.8 %grid_residuals.1.grid = f32[32,64,128]{2,1,0:T(8,128)} custom-call(f32[1,2,64,2048]{3,2,1,0:T(8,128)} %model.1, f32[1,64,2,256]{3,2,1,0:T(2,128)} %observed.1, f32[1,64,2,256]{3,2,1,0:T(2,128)} %coords.1, s32[1,1,64]{2,1,0:T(1,128)} %count.1, s32[1,1,64]{2,1,0:T(1,128)} %block.1, s32[1,1,64]{2,1,0:T(1,128)} %cell.1), custom_call_target="tpu_custom_call" | custom-call | tf_op jit(solution)/shard_map/grid_residuals/pallas_call | solution.py:387
  17.1 46.4 %image_and_sum.1 = f32[2,64,512]{2,1,0:T(8,128)} custom-call(f32[32,64,128]{2,1,0:T(8,128)} %grid_residuals.1.grid, f32[1,64,2048]{2,1,0:T(8,128)} %gain_in.1, s32[1]{0:T(128)S(6)} %copy.16.offset, s32[1]{0:T(128)S(6)} %copy.15.shift, s32[1,2]{1,0:T(1,128)} %tap_index.1, f32[8,5]{1,0:T(8,128)} %taps.1, bf16[32,128,192]{2,1,0:T(8,128)(2,1)} %constant.4.clone.row_table_in, ...), custom_call_target="tpu_custom_call" | custom-call | tf_op jit(solution)/shard_map/image_and_sum/pallas_call | solution.py:403
  63.5 1.7 %copy.17 = f32[2,64,512]{2,1,0:T(8,128)} copy(f32[2,64,512]{2,1,0:T(8,128)} %image_and_sum.1) | data formatting | bytes 524288

commit v4 on v3

--- a/solution.py
+++ b/solution.py
@@ -107,7 +107,7 @@
             windows[2 * pair + 1, rows, :] = jnp.where(left, swapped(high), low).astype(bf16)
         return carry
 
-    lax.fori_loop(0, NT // 2, prepare, 0)
+    lax.fori_loop(0, NT // 2, prepare, 0, unroll=8)
     grid[...] = jnp.zeros_like(grid)
     slot = lax.broadcasted_iota(jnp.int32, (2, SLOTS), 1)
 
@@ -131,11 +131,10 @@
         predicted = jnp.sum(rows.reshape(2, SIDE, SLOTS) * along_v[None], axis=1)
         residual = jnp.where(slot < count[0, 0, i], observed[0, k] - predicted, 0.0)
         weighted = jnp.concatenate([along_v * residual[0:1], along_v * residual[1:2]], axis=0)
-        high_w, low_w = split(weighted)
-        products = lax.dot_general(
+        high_w, low_w = split(weighted.T)
+        products = jnp.dot(
             jnp.concatenate([high_u, low_u], axis=0),
-            jnp.concatenate([high_w, low_w], axis=0),
-            (((1,), (1,)), ((), ())),
+            jnp.concatenate([high_w, low_w], axis=1),
             preferred_element_type=f32,
         )
         patch = products[:SIDE, : 2 * SIDE] + (
@@ -144,12 +143,12 @@
         return q, patch
 
     def several(i, carry):
-        done = [one(i * 4 + j) for j in range(4)]
+        done = [one(i * 32 + j) for j in range(32)]
         for q, patch in done:
             grid[q] += patch
         return carry
 
-    lax.fori_loop(0, SUBS // 4, several, 0)
+    lax.fori_loop(0, SUBS // 32, several, 0)
 
 
 def tail_kernel(

time: 65.6 us -> 57 us (0.87)
  Pallas kernels: 62.2 us -> 53.8 us
    pallas_call x1, Pallas kernels: 15.8 us -> 7.43 us  [gridded(): pl.pallas_call(grid_kernel, out_shape=jax.ShapeDtypeStruct((NT, SIDE, 2 *...]
where the time goes in v4:
time: 57 us; the launch traced here: 56.7 us
  Pallas kernels  53.8 us (94%)
  local copies, waits for them, and re-layouts  1.67 us (3%)
  between operations  1.31 us (2%)
    pallas_call x1, Pallas kernels, finished(): pl.pallas_call(tail_kernel, out_shape=jax.ShapeDtypeStruct((2, SIDE, CHUN...  46.3 us
    pallas_call x1, Pallas kernels, gridded(): pl.pallas_call(grid_kernel, out_shape=jax.ShapeDtypeStruct((NT, SIDE, 2 *...  7.43 us
    unnamed x1, local copies, waits for them, and re-layouts  1.67 us

profile of v4, /device:TPU:2, one launch (start us, length us, event | category | flops | bytes accessed | tf_op | source)
XLA Modules:
  0.0 56.7 jit_solution(12921253788094561356)
XLA Ops:
  1.3 7.4 %grid_residuals.1.grid = f32[32,64,128]{2,1,0:T(8,128)} custom-call(f32[1,2,64,2048]{3,2,1,0:T(8,128)} %model.1, f32[1,64,2,256]{3,2,1,0:T(2,128)} %observed.1, f32[1,64,2,256]{3,2,1,0:T(2,128)} %coords.1, s32[1,1,64]{2,1,0:T(1,128)} %count.1, s32[1,1,64]{2,1,0:T(1,128)} %block.1, s32[1,1,64]{2,1,0:T(1,128)} %cell.1), custom_call_target="tpu_custom_call" | custom-call | tf_op jit(solution)/shard_map/grid_residuals/pallas_call | solution.py:386
  8.7 46.3 %image_and_sum.1 = f32[2,64,512]{2,1,0:T(8,128)} custom-call(f32[32,64,128]{2,1,0:T(8,128)} %grid_residuals.1.grid, f32[1,64,2048]{2,1,0:T(8,128)} %gain_in.1, s32[1]{0:T(128)S(6)} %copy.16.offset, s32[1]{0:T(128)S(6)} %copy.15.shift, s32[1,2]{1,0:T(1,128)} %tap_index.1, f32[8,5]{1,0:T(8,128)} %taps.1, bf16[32,128,192]{2,1,0:T(8,128)(2,1)} %constant.4.clone.row_table_in, ...), custom_call_target="tpu_custom_call" | custom-call | tf_op jit(solution)/shard_map/image_and_sum/pallas_call | solution.py:402
  55.1 1.7 %copy.17 = f32[2,64,512]{2,1,0:T(8,128)} copy(f32[2,64,512]{2,1,0:T(8,128)} %image_and_sum.1) | data formatting | bytes 524288

commit v5 on v4

--- a/solution.py
+++ b/solution.py
@@ -220,13 +220,18 @@
             blocks[d, rows_of(g), :] = tapped[lax.rem(d - steps + NT, NT)]
             return carry
 
-        lax.fori_loop(0, NT, make, 0)
-        lax.fori_loop(0, NT, place, 0)
+        lax.fori_loop(0, NT, make, 0, unroll=8)
+        lax.fori_loop(0, NT, place, 0, unroll=8)
         landing[me, rows_of(g), :] = blocks[me, rows_of(g), :]
+
+    side, place_xy = me // 16, lax.rem(me, 16)
+
+    def peer_of(step):
+        return lax.rem(side + 1 + step, 2) * 16 + lax.rem(place_xy + step // 2, 16)
 
     def send_group(g):
         def send_one(step, inner):
-            peer = lax.rem(me + step, NT)
+            peer = peer_of(step)
             pltpu.make_async_remote_copy(
                 src_ref=blocks.at[peer, rows_of(g)],
                 dst_ref=landing.at[me, rows_of(g)],
@@ -237,7 +242,8 @@
             ).start()
             return inner
 
-        lax.fori_loop(1, NT, send_one, 0)
+        send_one(0, 0)
+        lax.fori_loop(2, NT, send_one, 0)
 
     make_group(0)
     pl.semaphore_wait(barrier, NT + 2)
@@ -385,7 +391,7 @@
 def gridded(model, observed, coords, count, block, cell):
     return pl.pallas_call(
         grid_kernel,
-        out_shape=jax.ShapeDtypeStruct((NT, SIDE, 2 * SIDE), f32),
+        out_shape=pltpu.VMEM((NT, SIDE, 2 * SIDE), f32),
         in_specs=[VMEM] * 3 + [SMEM] * 3,
         out_specs=VMEM,
         scratch_shapes=[
@@ -401,7 +407,7 @@
 def finished(grid, gain, offset, shift, tap_index, taps):
     return pl.pallas_call(
         tail_kernel,
-        out_shape=jax.ShapeDtypeStruct((2, SIDE, CHUNK), f32),
+        out_shape=pltpu.VMEM((2, SIDE, CHUNK), f32),
         in_specs=[VMEM, ANY] + [SMEM] * 4 + [ANY] * 2,
         out_specs=VMEM,
         scratch_shapes=[
@@ -443,6 +449,7 @@
     grid = gridded(
         model_grid, observed, coords, vis_count, subgrid_block, subgrid_cell,
     )
+    grid = pltpu.with_memory_space_constraint(grid, pltpu.VMEM)
     return finished(grid, beam_gain, row_offset, column_shift, interp_index, interp_taps)
 
 

time: 57 us -> 55.3 us (0.970)
  local copies, waits for them, and re-layouts: 1.67 us -> 0.71 us
  Pallas kernels: 53.8 us -> 53.2 us
    unnamed x1, local copies, waits for them, and re-layouts: 1.67 us -> 0.71 us
    pallas_call x2, Pallas kernels: 53.8 us -> 53.2 us  [the longest x1 46.8 us: finished(): pl.pallas_call(tail_kernel, out_shape=pltpu.VMEM((2, SIDE, CHUNK), f32),...]
where the time goes in v5:
time: 55.3 us; the launch traced here: 55.2 us
  Pallas kernels  53.2 us (96%)
  between operations  1.31 us (2%)
  local copies, waits for them, and re-layouts  0.71 us (1%)
    pallas_call x1, Pallas kernels, finished(): pl.pallas_call(tail_kernel, out_shape=pltpu.VMEM((2, SIDE, CHUNK), f32),...  46.8 us
    pallas_call x1, Pallas kernels, gridded(): pl.pallas_call(grid_kernel, out_shape=pltpu.VMEM((NT, SIDE, 2 * SIDE), f3...  6.41 us

profile of v5, /device:TPU:2, one launch (start us, length us, event | category | flops | bytes accessed | tf_op | source)
XLA Modules:
  0.0 55.2 jit_solution(15037816169151117988)
XLA Ops:
  1.3 6.4 %grid_residuals.1.grid = f32[32,64,128]{2,1,0:T(8,128)S(1)} custom-call(f32[1,2,64,2048]{3,2,1,0:T(8,128)} %model.1, f32[1,64,2,256]{3,2,1,0:T(2,128)} %observed.1, f32[1,64,2,256]{3,2,1,0:T(2,128)} %coords.1, s32[1,1,64]{2,1,0:T(1,128)} %count.1, s32[1,1,64]{2,1,0:T(1,128)} %block.1, s32[1,1,64]{2,1,0:T(1,128)} %cell.1), custom_call_target="tpu_custom_call" | custom-call | tf_op jit(solution)/shard_map/grid_residuals/pallas_call | solution.py:392
  7.7 46.8 %image_and_sum.1 = f32[2,64,512]{2,1,0:T(8,128)S(1)} custom-call(f32[32,64,128]{2,1,0:T(8,128)S(1)} %grid_residuals.1.grid, f32[1,64,2048]{2,1,0:T(8,128)} %gain_in.1, s32[1]{0:T(128)S(6)} %copy.17.offset, s32[1]{0:T(128)S(6)} %copy.16.shift, s32[1,2]{1,0:T(1,128)} %tap_index.1, f32[8,5]{1,0:T(8,128)} %taps.1, ...), custom_call_target="tpu_custom_call" | custom-call | tf_op jit(solution)/shard_map/image_and_sum/pallas_call | solution.py:408
  54.5 0.7 %copy.15 = f32[2,64,512]{2,1,0:T(8,128)} copy(f32[2,64,512]{2,1,0:T(8,128)S(1)} %image_and_sum.1) | data formatting | bytes 524288

commit v6 on v5

--- a/solution.py
+++ b/solution.py
@@ -186,22 +186,26 @@
                 spectrum[k, to, :] = value
             return carry
 
-        lax.fori_loop(0, rows // 8, tile, 0)
+        lax.fori_loop(0, rows // 8, tile, 0, unroll=4 if rows > 32 else 2)
 
     padded[pl.ds(0, PAD), :] = jnp.zeros((PAD, 2 * SIDE), f32)
     padded[pl.ds(PAD + G, PAD), :] = jnp.zeros((PAD, 2 * SIDE), f32)
     transform_rows(grid, 0, SIDE)
     row_copy.wait()
     wide_signs = lane_signs((SIDE, 2 * SIDE))
-    for x1 in range(NT):
+
+    def row_step(x1):
         high, low = split(spectrum[x1])
         both = jnp.dot(
             row_table[x1], jnp.concatenate([high, low, high], axis=0), preferred_element_type=f32
         )
         padded[pl.ds(PAD + x1, SIDE, stride=NT), :] = both[:SIDE] + swapped(both[SIDE:]) * wide_signs
 
+    def first_row(g):
+        return pl.multiple_of((lax.rem(g, 2) * 2 + g // 2) * ROWS, ROWS)
+
     def rows_of(g):
-        return pl.ds(pl.multiple_of(g * ROWS, ROWS), ROWS)
+        return pl.ds(first_row(g), ROWS)
 
     phase_x = tap_index[0, 0]
     weights_x = [taps[phase_x, tap] for tap in range(5)]
@@ -209,7 +213,7 @@
 
     def make_group(g):
         def make(d, carry):
-            start = pl.multiple_of(d * SIDE + g * ROWS, ROWS)
+            start = pl.multiple_of(d * SIDE + first_row(g), ROWS)
             total = weights_x[0] * padded[pl.ds(start + PAD + 2, ROWS), :]
             for tap in range(1, 5):
                 total = total + weights_x[tap] * padded[pl.ds(start + PAD + 2 - tap, ROWS), :]
@@ -245,19 +249,18 @@
         send_one(0, 0)
         lax.fori_loop(2, NT, send_one, 0)
 
+    for x1 in (*range(NT - 2, NT), *range(NT // 2 + 2)):
+        row_step(x1)
     make_group(0)
     pl.semaphore_wait(barrier, NT + 2)
-
-    def start_group(g, carry):
+    send_group(0)
+    make_group(1)
+    send_group(1)
+    for x1 in range(NT // 2 + 2, NT - 2):
+        row_step(x1)
+    for g in (2, 3):
+        make_group(g)
         send_group(g)
-
-        @pl.when(g < GROUPS - 1)
-        def _():
-            make_group(g + 1)
-
-        return carry
-
-    lax.fori_loop(0, GROUPS, start_group, 0)
     column_copy.wait()
     gain_copy.wait()
 
@@ -274,8 +277,8 @@
     kind = lax.broadcasted_iota(jnp.int32, (META, CHUNK), 0)
     facts = jnp.where(kind == 0, first, upper)
 
-    def image_group(g):
-        transform_rows(landing, g * ROWS, ROWS)
+    def start_image(g):
+        transform_rows(landing, first_row(g), ROWS)
         for y1 in range(NT):
             high, low = split(spectrum[y1, pl.ds(0, ROWS), :])
             both = lax.dot_general(
@@ -285,6 +288,8 @@
                 preferred_element_type=f32,
             )
             padded[pl.ds(PAD + y1, SIDE, stride=NT), pl.ds(0, ROWS)] = both[:SIDE] + both[SIDE:]
+
+    def finish_image(g):
         for part in range(G // 128):
             total = weights[0] * padded[pl.ds(part * 128 + PAD + 2, 128), :]
             for tap in range(1, 5):
@@ -349,23 +354,21 @@
 
     def group(g, carry):
         wait_group(g, tile_recv)
-        image_group(g)
-        pair(g).start()
+        start_image(g)
 
         @pl.when(g > 0)
         def _():
             first_hop(g - 1)
 
-        @pl.when(g > 1)
-        def _():
-            second_hop(g - 2)
+        finish_image(g)
+        pair(g).start()
 
         return carry
 
     lax.fori_loop(0, GROUPS, group, 0)
     first_hop(GROUPS - 1)
-    second_hop(GROUPS - 2)
-    second_hop(GROUPS - 1)
+    for g in range(GROUPS):
+        second_hop(g)
 
     def finish(g, carry):
         wait_group(g, tile_send)

time: 55.3 us -> 50.9 us (0.920)
  Pallas kernels: 53.2 us -> 48.7 us
    pallas_call x1, Pallas kernels: 46.8 us -> 42.3 us  [finished(): pl.pallas_call(tail_kernel, out_shape=pltpu.VMEM((2, SIDE, CHUNK), f32),...]
where the time goes in v6:
time: 50.9 us; the launch traced here: 50.7 us
  Pallas kernels  48.7 us (96%)
  between operations  1.31 us (3%)
  local copies, waits for them, and re-layouts  0.71 us (1%)
    pallas_call x1, Pallas kernels, finished(): pl.pallas_call(tail_kernel, out_shape=pltpu.VMEM((2, SIDE, CHUNK), f32),...  42.3 us
    pallas_call x1, Pallas kernels, gridded(): pl.pallas_call(grid_kernel, out_shape=pltpu.VMEM((NT, SIDE, 2 * SIDE), f3...  6.4 us

profile of v6, /device:TPU:2, one launch (start us, length us, event | category | flops | bytes accessed | tf_op | source)
XLA Modules:
  0.0 50.7 jit_solution(15555405130653314798)
XLA Ops:
  1.3 6.4 %grid_residuals.1.grid = f32[32,64,128]{2,1,0:T(8,128)S(1)} custom-call(f32[1,2,64,2048]{3,2,1,0:T(8,128)} %model.1, f32[1,64,2,256]{3,2,1,0:T(2,128)} %observed.1, f32[1,64,2,256]{3,2,1,0:T(2,128)} %coords.1, s32[1,1,64]{2,1,0:T(1,128)} %count.1, s32[1,1,64]{2,1,0:T(1,128)} %block.1, s32[1,1,64]{2,1,0:T(1,128)} %cell.1), custom_call_target="tpu_custom_call" | custom-call | tf_op jit(solution)/shard_map/grid_residuals/pallas_call | solution.py:395
  7.7 42.3 %image_and_sum.1 = f32[2,64,512]{2,1,0:T(8,128)S(1)} custom-call(f32[32,64,128]{2,1,0:T(8,128)S(1)} %grid_residuals.1.grid, f32[1,64,2048]{2,1,0:T(8,128)} %gain_in.1, s32[1]{0:T(128)S(6)} %copy.17.offset, s32[1]{0:T(128)S(6)} %copy.16.shift, s32[1,2]{1,0:T(1,128)} %tap_index.1, f32[8,5]{1,0:T(8,128)} %taps.1, ...), custom_call_target="tpu_custom_call" | custom-call | tf_op jit(solution)/shard_map/image_and_sum/pallas_call | solution.py:411
  50.0 0.7 %copy.15 = f32[2,64,512]{2,1,0:T(8,128)} copy(f32[2,64,512]{2,1,0:T(8,128)S(1)} %image_and_sum.1) | data formatting | bytes 524288

commit v7 on v6

--- a/solution.py
+++ b/solution.py
@@ -142,13 +142,8 @@
         )
         return q, patch
 
-    def several(i, carry):
-        done = [one(i * 32 + j) for j in range(32)]
-        for q, patch in done:
-            grid[q] += patch
-        return carry
-
-    lax.fori_loop(0, SUBS // 32, several, 0)
+    for q, patch in [one(i) for i in range(SUBS)]:
+        grid[q] += patch
 
 
 def tail_kernel(
@@ -277,9 +272,8 @@
     kind = lax.broadcasted_iota(jnp.int32, (META, CHUNK), 0)
     facts = jnp.where(kind == 0, first, upper)
 
-    def start_image(g):
-        transform_rows(landing, first_row(g), ROWS)
-        for y1 in range(NT):
+    def column_steps(first, last):
+        for y1 in range(first, last):
             high, low = split(spectrum[y1, pl.ds(0, ROWS), :])
             both = lax.dot_general(
                 table[y1],
@@ -354,12 +348,14 @@
 
     def group(g, carry):
         wait_group(g, tile_recv)
-        start_image(g)
+        transform_rows(landing, first_row(g), ROWS)
+        column_steps(0, NT // 2)
 
         @pl.when(g > 0)
         def _():
             first_hop(g - 1)
 
+        column_steps(NT // 2, NT)
         finish_image(g)
         pair(g).start()
 

time: 50.9 us -> 50.3 us (0.988)
  no operation moved by 1% of the time
where the time goes in v7:
time: 50.3 us; the launch traced here: 50.2 us
  Pallas kernels  48.2 us (96%)
  between operations  1.31 us (3%)
  local copies, waits for them, and re-layouts  0.71 us (1%)
    pallas_call x1, Pallas kernels, finished(): pl.pallas_call(tail_kernel, out_shape=pltpu.VMEM((2, SIDE, CHUNK), f32),...  42 us
    pallas_call x1, Pallas kernels, gridded(): pl.pallas_call(grid_kernel, out_shape=pltpu.VMEM((NT, SIDE, 2 * SIDE), f3...  6.2 us

profile of v7, /device:TPU:2, one launch (start us, length us, event | category | flops | bytes accessed | tf_op | source)
XLA Modules:
  0.0 50.2 jit_solution(10406311343460356197)
XLA Ops:
  1.3 6.2 %grid_residuals.1.grid = f32[32,64,128]{2,1,0:T(8,128)S(1)} custom-call(f32[1,2,64,2048]{3,2,1,0:T(8,128)} %model.1, f32[1,64,2,256]{3,2,1,0:T(2,128)} %observed.1, f32[1,64,2,256]{3,2,1,0:T(2,128)} %coords.1, s32[1,1,64]{2,1,0:T(1,128)} %count.1, s32[1,1,64]{2,1,0:T(1,128)} %block.1, s32[1,1,64]{2,1,0:T(1,128)} %cell.1), custom_call_target="tpu_custom_call" | custom-call | tf_op jit(solution)/shard_map/grid_residuals/pallas_call | solution.py:391
  7.5 42.0 %image_and_sum.1 = f32[2,64,512]{2,1,0:T(8,128)S(1)} custom-call(f32[32,64,128]{2,1,0:T(8,128)S(1)} %grid_residuals.1.grid, f32[1,64,2048]{2,1,0:T(8,128)} %gain_in.1, s32[1]{0:T(128)S(6)} %copy.17.offset, s32[1]{0:T(128)S(6)} %copy.16.shift, s32[1,2]{1,0:T(1,128)} %tap_index.1, f32[8,5]{1,0:T(8,128)} %taps.1, ...), custom_call_target="tpu_custom_call" | custom-call | tf_op jit(solution)/shard_map/image_and_sum/pallas_call | solution.py:407
  49.5 0.7 %copy.15 = f32[2,64,512]{2,1,0:T(8,128)} copy(f32[2,64,512]{2,1,0:T(8,128)S(1)} %image_and_sum.1) | data formatting | bytes 524288

commit v8 on v7

--- a/solution.py
+++ b/solution.py
@@ -157,6 +157,8 @@
     level, core = beam // 2, lax.rem(beam, 2)
     mate = beam + 1 - 2 * core
     up, down = lax.rem(beam + 2, BEAMS), lax.rem(beam + 6, BEAMS)
+    row_copy = pltpu.make_async_copy(row_table_in, row_table, in_sem.at[0])
+    row_copy.start()
     barrier = pltpu.get_barrier_semaphore()
     for step in range(1, NT):
         pl.semaphore_signal(
@@ -164,13 +166,6 @@
         )
     for peer in (mate, up, down):
         pl.semaphore_signal(barrier, inc=1, device_id={"beam": peer}, device_id_type=MESH)
-    row_copy = pltpu.make_async_copy(row_table_in, row_table, in_sem.at[0])
-    row_copy.start()
-    column_copy = pltpu.make_async_copy(table_in, table, in_sem.at[1])
-    column_copy.start()
-    gain_copy = pltpu.make_async_copy(gain_in, gain, in_sem.at[2])
-    gain_copy.start()
-
     signs = lane_signs((8, 2 * SIDE))
 
     def transform_rows(source, start, rows):
@@ -187,6 +182,10 @@
     padded[pl.ds(PAD + G, PAD), :] = jnp.zeros((PAD, 2 * SIDE), f32)
     transform_rows(grid, 0, SIDE)
     row_copy.wait()
+    column_copy = pltpu.make_async_copy(table_in, table, in_sem.at[1])
+    column_copy.start()
+    gain_copy = pltpu.make_async_copy(gain_in, gain, in_sem.at[2])
+    gain_copy.start()
     wide_signs = lane_signs((SIDE, 2 * SIDE))
 
     def row_step(x1):
@@ -219,8 +218,8 @@
             blocks[d, rows_of(g), :] = tapped[lax.rem(d - steps + NT, NT)]
             return carry
 
-        lax.fori_loop(0, NT, make, 0, unroll=8)
-        lax.fori_loop(0, NT, place, 0, unroll=8)
+        lax.fori_loop(0, NT, make, 0, unroll=16)
+        lax.fori_loop(0, NT, place, 0, unroll=16)
         landing[me, rows_of(g), :] = blocks[me, rows_of(g), :]
 
     side, place_xy = me // 16, lax.rem(me, 16)
@@ -242,7 +241,7 @@
             return inner
 
         send_one(0, 0)
-        lax.fori_loop(2, NT, send_one, 0)
+        lax.fori_loop(2, NT, send_one, 0, unroll=10)
 
     for x1 in (*range(NT - 2, NT), *range(NT // 2 + 2)):
         row_step(x1)

time: 50.3 us -> 50.7 us (level)
  the two profiles are of different devices: /device:TPU:2 before, /device:TPU:33 now
where the time goes in v8:
time: 50.7 us; the launch traced here: 50.4 us
  Pallas kernels  48.4 us (95%)
  between operations  1.31 us (3%)
  local copies, waits for them, and re-layouts  0.71 us (1%)
    pallas_call x1, Pallas kernels, finished(): pl.pallas_call(tail_kernel, out_shape=pltpu.VMEM((2, SIDE, CHUNK), f32),...  42.2 us
    pallas_call x1, Pallas kernels, gridded(): pl.pallas_call(grid_kernel, out_shape=pltpu.VMEM((NT, SIDE, 2 * SIDE), f3...  6.21 us

profile of v8, /device:TPU:33, one launch (start us, length us, event | category | flops | bytes accessed | tf_op | source)
XLA Modules:
  0.0 50.4 jit_solution(14212326830662321877)
XLA Ops:
  1.3 6.2 %grid_residuals.1.grid = f32[32,64,128]{2,1,0:T(8,128)S(1)} custom-call(f32[1,2,64,2048]{3,2,1,0:T(8,128)} %model.1, f32[1,64,2,256]{3,2,1,0:T(2,128)} %observed.1, f32[1,64,2,256]{3,2,1,0:T(2,128)} %coords.1, s32[1,1,64]{2,1,0:T(1,128)} %count.1, s32[1,1,64]{2,1,0:T(1,128)} %block.1, s32[1,1,64]{2,1,0:T(1,128)} %cell.1), custom_call_target="tpu_custom_call" | custom-call | tf_op jit(solution)/shard_map/grid_residuals/pallas_call | solution.py:390
  7.5 42.2 %image_and_sum.1 = f32[2,64,512]{2,1,0:T(8,128)S(1)} custom-call(f32[32,64,128]{2,1,0:T(8,128)S(1)} %grid_residuals.1.grid, f32[1,64,2048]{2,1,0:T(8,128)} %gain_in.1, s32[1]{0:T(128)S(6)} %copy.17.offset, s32[1]{0:T(128)S(6)} %copy.16.shift, s32[1,2]{1,0:T(1,128)} %tap_index.1, f32[8,5]{1,0:T(8,128)} %taps.1, ...), custom_call_target="tpu_custom_call" | custom-call | tf_op jit(solution)/shard_map/image_and_sum/pallas_call | solution.py:406
  49.7 0.7 %copy.15 = f32[2,64,512]{2,1,0:T(8,128)} copy(f32[2,64,512]{2,1,0:T(8,128)S(1)} %image_and_sum.1) | data formatting | bytes 524288
